TPU v7x, 512 devices: a whole 4x8x8 slice. The times are simulated.
512 devices in a mesh: prompt: 8 (over y), resp: 64 (over z, x, core).
Axes of the slice: x: 4, y: 8, z: 8, core: 2. Of those that a mesh axis runs over, the one named last changes fastest.
Arguments:
- queries: bfloat16 [8, 64, 256, 2048], P('prompt', 'resp')
- resp_kv: bfloat16 [8, 64, 256, 1024], P('prompt', 'resp')
- out_grad: bfloat16 [8, 64, 256, 2048], P('prompt', 'resp'), may hold values from -6 to 6
- prompt_kv: bfloat16 [64, 128, 1024], P('resp', 'prompt'), may hold values from -6 to 6
- prompt_of: int32 [64], replicated, may hold values from 0 to 63, as said below
- lengths: int32 [8, 64], P('prompt', 'resp'), may hold values from 1 to 2
Outputs:
- query_grad: bfloat16 [8, 64, 256, 2048], P('prompt', 'resp')
- resp_kv_grad: bfloat16 [8, 64, 256, 1024], P('prompt', 'resp')
- prompt_kv_grad: float32 [64, 128, 1024], P('resp', 'prompt')
Inputs may be any that keep to these rules, and one draw needn't show every extreme that they name: The cyclic distance between b and prompt_of[b] (mod 64) is at most 3; it is 3 on both sides for some b.
All inputs are finite; a program needn't handle non-finite values.
Results may differ from a plain program's by a relative error of at most 0.024.
Values may be sent and summed in bfloat16 or wider, within the bound.
A program may use at most 64 MiB of HBM per device.

v0:
```python
import jax
import jax.numpy as jnp
from jax import lax
from jax.sharding import PartitionSpec as P

QH = 16
KVH = 4
HD = 128
BLOCK = 128
REACH = 3


masked_value = -1e30


def from_behind(value, axis, steps):
    count = lax.axis_size(axis)
    pairs = [(source, (source + steps) % count) for source in range(count)]
    return lax.ppermute(value, axis, pairs)


def shards(queries, resp_kv, out_grad, prompt_kv, prompt_of, lengths):
    groups = QH // KVH
    softmax_scale = HD ** (-0.5)
    key_width = KVH * HD
    column = lax.axis_index("resp")
    group_size = lax.axis_size("resp")
    wanted = prompt_of[column]
    offset = (column - wanted + group_size + REACH) % group_size - REACH
    own_rows = prompt_kv[0]
    full_rows = lax.all_gather(own_rows, "prompt", axis=0, tiled=True)
    fetched = jnp.where(offset == 0, full_rows, jnp.zeros_like(full_rows))
    for stride in range(1, REACH + 1):
        for signed in (stride, -stride):
            arrived = from_behind(full_rows, "resp", signed)
            fetched = jnp.where(offset == signed, arrived, fetched)
    query_rows = queries[0, 0]
    resp_rows = resp_kv[0, 0]
    grad_rows = out_grad[0, 0]
    resp_len = query_rows.shape[0]
    row_index = jnp.arange(resp_len, dtype=jnp.int32)
    live_rows = row_index < lengths[0, 0] * BLOCK
    masked_grad = jnp.where(live_rows[:, None], grad_rows, jnp.zeros_like(grad_rows))
    causal = row_index[None, :] <= row_index[:, None]
    query_parts = []
    resp_key_parts = []
    resp_value_parts = []
    prompt_key_parts = []
    prompt_value_parts = []
    for head_index in range(KVH):
        query_slice = slice(head_index * groups * HD, (head_index + 1) * groups * HD)
        key_slice = slice(head_index * HD, (head_index + 1) * HD)
        value_slice = slice(key_width + head_index * HD, key_width + (head_index + 1) * HD)
        query_head_block = query_rows[:, query_slice].reshape(resp_len, groups, HD)
        head_gradient = masked_grad[:, query_slice].reshape(resp_len, groups, HD)
        prompt_key_block = fetched[:, key_slice]
        prompt_value_block = fetched[:, value_slice]
        response_key_block = resp_rows[:, key_slice]
        response_value_block = resp_rows[:, value_slice]
        score_resp = (
            jnp.einsum(
                "xjc,bc->jxb",
                query_head_block,
                response_key_block,
                preferred_element_type=jnp.float32,
            )
            * softmax_scale
        )
        score_resp = jnp.where(causal[None], score_resp, masked_value)
        score_prompt = (
            jnp.einsum(
                "xjc,bc->jxb",
                query_head_block,
                prompt_key_block,
                preferred_element_type=jnp.float32,
            )
            * softmax_scale
        )
        top_score = jnp.maximum(
            jnp.max(score_prompt, axis=-1, keepdims=True),
            jnp.max(score_resp, axis=-1, keepdims=True),
        )
        exp_prompt = jnp.exp(score_prompt - top_score)
        exp_resp = jnp.exp(score_resp - top_score)
        total_mass = jnp.sum(exp_prompt, axis=-1, keepdims=True) + jnp.sum(
            exp_resp, axis=-1, keepdims=True
        )
        prob_prompt = exp_prompt / total_mass
        prob_resp = exp_resp / total_mass
        prompt_round_block = prob_prompt.astype(jnp.bfloat16)
        response_round_block = prob_resp.astype(jnp.bfloat16)
        head_out = jnp.einsum(
            "czu,uk->zck",
            prompt_round_block,
            prompt_value_block,
            preferred_element_type=jnp.float32,
        )
        head_out = head_out + jnp.einsum(
            "czu,uk->zck",
            response_round_block,
            response_value_block,
            preferred_element_type=jnp.float32,
        )
        head_out = head_out.astype(jnp.bfloat16)
        row_delta = jnp.sum(
            head_gradient.astype(jnp.float32) * head_out.astype(jnp.float32), axis=-1
        )
        row_delta = jnp.transpose(row_delta, (1, 0))[..., None]
        back_prompt = jnp.einsum(
            "xjc,bc->jxb", head_gradient, prompt_value_block, preferred_element_type=jnp.float32
        )
        back_resp = jnp.einsum(
            "xjc,bc->jxb", head_gradient, response_value_block, preferred_element_type=jnp.float32
        )
        prompt_score_gradient = (prob_prompt * (back_prompt - row_delta)).astype(jnp.bfloat16)
        response_score_gradient = (prob_resp * (back_resp - row_delta)).astype(jnp.bfloat16)
        query_head_grad = jnp.einsum(
            "czu,uk->zck",
            prompt_score_gradient,
            prompt_key_block,
            preferred_element_type=jnp.float32,
        )
        query_head_grad = query_head_grad + jnp.einsum(
            "czu,uk->zck",
            response_score_gradient,
            response_key_block,
            preferred_element_type=jnp.float32,
        )
        query_parts.append(
            (query_head_grad * softmax_scale).astype(jnp.bfloat16).reshape(resp_len, groups * HD)
        )
        prompt_key_parts.append(
            jnp.einsum(
                "lpb,ply->by",
                prompt_score_gradient,
                query_head_block,
                preferred_element_type=jnp.float32,
            )
            * softmax_scale
        )
        prompt_value_parts.append(
            jnp.einsum(
                "lpb,ply->by", prompt_round_block, head_gradient, preferred_element_type=jnp.float32
            )
        )
        resp_key_parts.append(
            jnp.einsum(
                "lpb,ply->by",
                response_score_gradient,
                query_head_block,
                preferred_element_type=jnp.float32,
            )
            * softmax_scale
        )
        resp_value_parts.append(
            jnp.einsum(
                "lpb,ply->by",
                response_round_block,
                head_gradient,
                preferred_element_type=jnp.float32,
            )
        )
    query_grad = jnp.concatenate(query_parts, axis=1)
    resp_grad = jnp.concatenate(resp_key_parts + resp_value_parts, axis=1).astype(jnp.bfloat16)
    prompt_partial = jnp.concatenate(prompt_key_parts + prompt_value_parts, axis=1)
    rows_sum = lax.psum_scatter(prompt_partial, "prompt", scatter_dimension=0, tiled=True)
    collected = jnp.where(wanted == column, rows_sum, jnp.zeros_like(rows_sum))
    for stride in range(1, REACH + 1):
        for signed in (stride, -stride):
            arrived = from_behind(rows_sum.astype(jnp.bfloat16), "resp", -signed).astype(
                rows_sum.dtype
            )
            source = (column + signed + group_size) % group_size
            collected = collected + jnp.where(
                prompt_of[source] == column, arrived, jnp.zeros_like(arrived)
            )
    return (query_grad[None, None], resp_grad[None, None], collected[None])


def solution(mesh):
    return jax.shard_map(
        shards,
        mesh=mesh,
        in_specs=(
            P("prompt", "resp", None, None),
            P("prompt", "resp", None, None),
            P("prompt", "resp", None, None),
            P("resp", "prompt", None),
            P(),
            P("prompt", "resp"),
        ),
        out_specs=(
            P("prompt", "resp", None, None),
            P("prompt", "resp", None, None),
            P("resp", "prompt", None),
        ),
        check_vma=False,
    )
```

profile of v0, /device:TPU:1, one launch (start us, length us, event | category | flops | bytes accessed | tf_op | source)
XLA Modules:
  0.0 189.1 jit_solution(11302706265438290318)
XLA Ops:
  7.2 23.1 %all-gather = bf16[1,128,1024]{2,1,0:T(8,128)(2,1)} all-gather(bf16[1,16,1024]{2,1,0:T(8,128)(2,1)} %param.9), channel_id=2, replica_groups=mesh['prompt'=8,'resp'=64] {'prompt'}, dimensions={1}, use_global_device_ids=true | all-gather | bytes 294912 | tf_op jit(solution)/shard_map/all_gather | solution.py:31
  30.3 10.1 %collective-permute-start.5 = (bf16[128,1024]{1,0:T(8,128)(2,1)}, bf16[128,1024]{1,0:T(8,128)(2,1)}, u32[]{:S(2)}, u32[]{:S(2)}) collective-permute-start(bf16[128,1024]{1,0:T(8,128)(2,1)} %bitcast.1), channel_id=1, source_target_pairs={{0,1},{1,2},{2,3},{3,4},{4,5},{5,6},{6,7},{7,8},{8,9},{9,10},{10,1... | collective-permute-start | bytes 786440 | tf_op jit(solution)/shard_map/ppermute | solution.py:19
  40.4 4.5 %collective-permute-start.4 = (bf16[128,1024]{1,0:T(8,128)(2,1)}, bf16[128,1024]{1,0:T(8,128)(2,1)}, u32[]{:S(2)}, u32[]{:S(2)}) collective-permute-start(bf16[128,1024]{1,0:T(8,128)(2,1)} %bitcast.1), channel_id=1, source_target_pairs={{0,63},{1,0},{2,1},{3,2},{4,3},{5,4},{6,5},{7,6},{8,7},{9,8},{10,9... | collective-permute-start | bytes 786440 | tf_op jit(solution)/shard_map/ppermute | solution.py:19
  44.9 1.9 %collective-permute-start.3 = (bf16[128,1024]{1,0:T(8,128)(2,1)}, bf16[128,1024]{1,0:T(8,128)(2,1)}, u32[]{:S(2)}, u32[]{:S(2)}) collective-permute-start(bf16[128,1024]{1,0:T(8,128)(2,1)} %bitcast.1), channel_id=1, source_target_pairs={{0,2},{1,3},{2,4},{3,5},{4,6},{5,7},{6,8},{7,9},{8,10},{9,11},{10,... | collective-permute-start | bytes 786440 | tf_op jit(solution)/shard_map/ppermute | solution.py:19
  46.9 9.2 %collective-permute-start.2 = (bf16[128,1024]{1,0:T(8,128)(2,1)}, bf16[128,1024]{1,0:T(8,128)(2,1)}, u32[]{:S(2)}, u32[]{:S(2)}) collective-permute-start(bf16[128,1024]{1,0:T(8,128)(2,1)} %bitcast.1), channel_id=1, source_target_pairs={{0,62},{1,63},{2,0},{3,1},{4,2},{5,3},{6,4},{7,5},{8,6},{9,7},{10,... | collective-permute-start | bytes 786440 | tf_op jit(solution)/shard_map/ppermute | solution.py:19
  56.1 1.9 %collective-permute-start.1 = (bf16[128,1024]{1,0:T(8,128)(2,1)}, bf16[128,1024]{1,0:T(8,128)(2,1)}, u32[]{:S(2)}, u32[]{:S(2)}) collective-permute-start(bf16[128,1024]{1,0:T(8,128)(2,1)} %bitcast.1), channel_id=1, source_target_pairs={{0,3},{1,4},{2,5},{3,6},{4,7},{5,8},{6,9},{7,10},{8,11},{9,12},{10... | collective-permute-start | bytes 786440 | tf_op jit(solution)/shard_map/ppermute | solution.py:19
  58.8 1.5 copy.167
  61.1 1.6 copy.170
  62.8 1.0 fusion.141
  63.8 1.1 fusion.144
  65.0 1.2 fusion.150
  68.2 1.3 fusion.146
  69.5 7.1 %collective-permute-start = (bf16[128,1024]{1,0:T(8,128)(2,1)}, bf16[128,1024]{1,0:T(8,128)(2,1)}, u32[]{:S(2)}, u32[]{:S(2)}) collective-permute-start(bf16[128,1024]{1,0:T(8,128)(2,1)} %bitcast.1), channel_id=1, source_target_pairs={{0,61},{1,62},{2,63},{3,0},{4,1},{5,2},{6,3},{7,4},{8,5},{9,6},{10... | collective-permute-start | bytes 786440 | tf_op jit(solution)/shard_map/ppermute | solution.py:19
  80.3 1.3 fusion.148
  81.7 1.1 select_select_fusion
  95.3 1.0 fusion.50
  97.8 1.0 fusion.48
  99.6 1.0 fusion.46
  106.7 2.1 %copy.327 = f32[128,1024]{1,0:T(8,128)} copy(f32[128,1024]{0,1:T(8,128)} %fusion.96) | data formatting | bytes 1048576
  109.8 1.9 copy.224
  117.1 1.1 maximum_bitcast_fusion
  118.2 26.8 %reduce-scatter.4.cloned.1.call-done = f32[16,1024]{1,0:T(8,128)} async-done(((f32[128,1024]{1,0:T(8,128)}), f32[16,1024]{1,0:T(8,128)}) %reduce-scatter.4.cloned.1.call-update) | async-done | bytes 65552
  145.0 1.0 copy.328
  146.1 10.1 %collective-permute-start.11 = (bf16[16,1024]{0,1:T(8,128)(2,1)S(1)}, bf16[16,1024]{0,1:T(8,128)(2,1)S(1)}, u32[]{:S(2)}, u32[]{:S(2)}) collective-permute-start(bf16[16,1024]{0,1:T(8,128)(2,1)S(1)} %convert_element_type.162), channel_id=1, source_target_pairs={{0,3},{1,4},{2,5},{3,6},{4,7},{5,8},{6,9},{7,10},{8,11},{9,12},{10... | collective-permute-start | bytes 98312 | tf_op jit(solution)/shard_map/ppermute | solution.py:19
  156.5 5.0 %collective-permute-start.10 = (bf16[16,1024]{0,1:T(8,128)(2,1)S(1)}, bf16[16,1024]{0,1:T(8,128)(2,1)S(1)}, u32[]{:S(2)}, u32[]{:S(2)}) collective-permute-start(bf16[16,1024]{0,1:T(8,128)(2,1)S(1)} %convert_element_type.162), channel_id=1, source_target_pairs={{0,61},{1,62},{2,63},{3,0},{4,1},{5,2},{6,3},{7,4},{8,5},{9,6},{10... | collective-permute-start | bytes 98312 | tf_op jit(solution)/shard_map/ppermute | solution.py:19
  161.5 1.9 %collective-permute-start.9 = (bf16[16,1024]{0,1:T(8,128)(2,1)S(1)}, bf16[16,1024]{0,1:T(8,128)(2,1)S(1)}, u32[]{:S(2)}, u32[]{:S(2)}) collective-permute-start(bf16[16,1024]{0,1:T(8,128)(2,1)S(1)} %convert_element_type.162), channel_id=1, source_target_pairs={{0,2},{1,3},{2,4},{3,5},{4,6},{5,7},{6,8},{7,9},{8,10},{9,11},{10,... | collective-permute-start | bytes 98312 | tf_op jit(solution)/shard_map/ppermute | solution.py:19
  163.4 6.7 %collective-permute-start.8 = (bf16[16,1024]{0,1:T(8,128)(2,1)S(1)}, bf16[16,1024]{0,1:T(8,128)(2,1)S(1)}, u32[]{:S(2)}, u32[]{:S(2)}) collective-permute-start(bf16[16,1024]{0,1:T(8,128)(2,1)S(1)} %convert_element_type.162), channel_id=1, source_target_pairs={{0,62},{1,63},{2,0},{3,1},{4,2},{5,3},{6,4},{7,5},{8,6},{9,7},{10,... | collective-permute-start | bytes 98312 | tf_op jit(solution)/shard_map/ppermute | solution.py:19
  170.1 1.9 %collective-permute-start.7 = (bf16[16,1024]{0,1:T(8,128)(2,1)S(1)}, bf16[16,1024]{0,1:T(8,128)(2,1)S(1)}, u32[]{:S(2)}, u32[]{:S(2)}) collective-permute-start(bf16[16,1024]{0,1:T(8,128)(2,1)S(1)} %convert_element_type.162), channel_id=1, source_target_pairs={{0,1},{1,2},{2,3},{3,4},{4,5},{5,6},{6,7},{7,8},{8,9},{9,10},{10,1... | collective-permute-start | bytes 98312 | tf_op jit(solution)/shard_map/ppermute | solution.py:19
  172.1 2.4 %collective-permute-start.6 = (bf16[16,1024]{0,1:T(8,128)(2,1)S(1)}, bf16[16,1024]{0,1:T(8,128)(2,1)}, u32[]{:S(2)}, u32[]{:S(2)}) collective-permute-start(bf16[16,1024]{0,1:T(8,128)(2,1)S(1)} %convert_element_type.162), channel_id=1, source_target_pairs={{0,63},{1,0},{2,1},{3,2},{4,3},{5,4},{6,5},{7,6},{8,7},{9,8},{10,9... | collective-permute-start | bytes 98312 | tf_op jit(solution)/shard_map/ppermute | solution.py:19
  174.8 1.0 copy.241
  176.6 3.5 %collective-permute-done.6 = bf16[16,1024]{0,1:T(8,128)(2,1)} collective-permute-done((bf16[16,1024]{0,1:T(8,128)(2,1)S(1)}, bf16[16,1024]{0,1:T(8,128)(2,1)}, u32[]{:S(2)}, u32[]{:S(2)}) %collective-permute-start.6) | collective-permute-done | bytes 32800 | tf_op jit(solution)/shard_map/ppermute | solution.py:19
  180.1 1.4 add_bitcast_fusion
  (140 shorter events, 31.0 us)
Async XLA Ops:
  7.2 137.8 %reduce-scatter.4.cloned.1.call-start = ((), (), s32[]{:S(2)}) async-start(), calls=%async_computation.1 | async-start | bytes 589824
  30.3 39.2 %collective-permute-start.5 = (bf16[128,1024]{1,0:T(8,128)(2,1)}, bf16[128,1024]{1,0:T(8,128)(2,1)}, u32[]{:S(2)}, u32[]{:S(2)}) collective-permute-start(bf16[128,1024]{1,0:T(8,128)(2,1)} %bitcast.1), channel_id=1, source_target_pairs={{0,1},{1,2},{2,3},{3,4},{4,5},{5,6},{6,7},{7,8},{8,9},{9,10},{10,1... | collective-permute-start | bytes 786440 | tf_op jit(solution)/shard_map/ppermute | solution.py:19
  40.4 41.2 %collective-permute-start.4 = (bf16[128,1024]{1,0:T(8,128)(2,1)}, bf16[128,1024]{1,0:T(8,128)(2,1)}, u32[]{:S(2)}, u32[]{:S(2)}) collective-permute-start(bf16[128,1024]{1,0:T(8,128)(2,1)} %bitcast.1), channel_id=1, source_target_pairs={{0,63},{1,0},{2,1},{3,2},{4,3},{5,4},{6,5},{7,6},{8,7},{9,8},{10,9... | collective-permute-start | bytes 786440 | tf_op jit(solution)/shard_map/ppermute | solution.py:19
  44.9 36.7 %collective-permute-start.3 = (bf16[128,1024]{1,0:T(8,128)(2,1)}, bf16[128,1024]{1,0:T(8,128)(2,1)}, u32[]{:S(2)}, u32[]{:S(2)}) collective-permute-start(bf16[128,1024]{1,0:T(8,128)(2,1)} %bitcast.1), channel_id=1, source_target_pairs={{0,2},{1,3},{2,4},{3,5},{4,6},{5,7},{6,8},{7,9},{8,10},{9,11},{10,... | collective-permute-start | bytes 786440 | tf_op jit(solution)/shard_map/ppermute | solution.py:19
  46.9 34.8 %collective-permute-start.2 = (bf16[128,1024]{1,0:T(8,128)(2,1)}, bf16[128,1024]{1,0:T(8,128)(2,1)}, u32[]{:S(2)}, u32[]{:S(2)}) collective-permute-start(bf16[128,1024]{1,0:T(8,128)(2,1)} %bitcast.1), channel_id=1, source_target_pairs={{0,62},{1,63},{2,0},{3,1},{4,2},{5,3},{6,4},{7,5},{8,6},{9,7},{10,... | collective-permute-start | bytes 786440 | tf_op jit(solution)/shard_map/ppermute | solution.py:19
  56.1 25.6 %collective-permute-start.1 = (bf16[128,1024]{1,0:T(8,128)(2,1)}, bf16[128,1024]{1,0:T(8,128)(2,1)}, u32[]{:S(2)}, u32[]{:S(2)}) collective-permute-start(bf16[128,1024]{1,0:T(8,128)(2,1)} %bitcast.1), channel_id=1, source_target_pairs={{0,3},{1,4},{2,5},{3,6},{4,7},{5,8},{6,9},{7,10},{8,11},{9,12},{10... | collective-permute-start | bytes 786440 | tf_op jit(solution)/shard_map/ppermute | solution.py:19
  61.1 3.8 %copy-start.3 = (bf16[256,512]{0,1:T(8,128)(2,1)}, bf16[256,512]{0,1:T(8,128)(2,1)S(1)}, u32[]{:S(2)}) copy-start(bf16[256,512]{0,1:T(8,128)(2,1)S(1)} %get-tuple-element.12) | copy-start | bytes 786436
  64.9 1.2 copy-start.27
  69.5 12.1 %collective-permute-start = (bf16[128,1024]{1,0:T(8,128)(2,1)}, bf16[128,1024]{1,0:T(8,128)(2,1)}, u32[]{:S(2)}, u32[]{:S(2)}) collective-permute-start(bf16[128,1024]{1,0:T(8,128)(2,1)} %bitcast.1), channel_id=1, source_target_pairs={{0,61},{1,62},{2,63},{3,0},{4,1},{5,2},{6,3},{7,4},{8,5},{9,6},{10... | collective-permute-start | bytes 786440 | tf_op jit(solution)/shard_map/ppermute | solution.py:19
  81.6 1.4 copy-start.4
  86.6 7.6 %copy-start.7 = (bf16[4,256,256]{1,2,0:T(8,128)(2,1)}, bf16[4,256,256]{1,2,0:T(8,128)(2,1)S(1)}, u32[]{:S(2)}) copy-start(bf16[4,256,256]{1,2,0:T(8,128)(2,1)S(1)} %fusion.16) | copy-start | bytes 1572868
  106.7 2.1 %copy-start.1 = (bf16[256,512]{0,1:T(8,128)(2,1)S(1)}, bf16[256,512]{0,1:T(8,128)(2,1)}, u32[]{:S(2)}) copy-start(bf16[256,512]{0,1:T(8,128)(2,1)} %get-tuple-element.14) | copy-start | bytes 786436
  108.8 2.9 %copy-start.10 = (bf16[256,4,128]{0,2,1:T(8,128)(2,1)S(1)}, bf16[256,4,128]{0,2,1:T(8,128)(2,1)}, u32[]{:S(2)}) copy-start(bf16[256,4,128]{0,2,1:T(8,128)(2,1)} %fusion.50) | copy-start | bytes 786436
  108.8 4.6 %copy-start.11 = (bf16[256,4,128]{0,2,1:T(8,128)(2,1)S(1)}, bf16[256,4,128]{0,2,1:T(8,128)(2,1)}, u32[]{:S(2)}) copy-start(bf16[256,4,128]{0,2,1:T(8,128)(2,1)} %fusion.48) | copy-start | bytes 786436
  109.8 2.8 %copy-start.12 = (bf16[256,4,128]{0,2,1:T(8,128)(2,1)S(1)}, bf16[256,4,128]{0,2,1:T(8,128)(2,1)}, u32[]{:S(2)}) copy-start(bf16[256,4,128]{0,2,1:T(8,128)(2,1)} %fusion.46) | copy-start | bytes 786436
  109.8 4.5 %copy-start.8 = (bf16[4,256,256]{1,2,0:T(8,128)(2,1)S(1)}, bf16[4,256,256]{1,2,0:T(8,128)(2,1)}, u32[]{:S(2)}) copy-start(bf16[4,256,256]{1,2,0:T(8,128)(2,1)} %copy-done.7) | copy-start | bytes 1572868
  112.5 2.7 %copy-start.20 = (bf16[256,512]{0,1:T(8,128)(2,1)S(1)}, bf16[256,512]{0,1:T(8,128)(2,1)}, u32[]{:S(2)}) copy-start(bf16[256,512]{0,1:T(8,128)(2,1)} %get-tuple-element.16) | copy-start | bytes 786436
  113.4 2.8 %copy-start.18 = (bf16[256,512]{0,1:T(8,128)(2,1)S(1)}, bf16[256,512]{0,1:T(8,128)(2,1)}, u32[]{:S(2)}) copy-start(bf16[256,512]{0,1:T(8,128)(2,1)} %get-tuple-element.19) | copy-start | bytes 786436
  115.2 1.9 %copy-start.21 = (bf16[256,512]{1,0:T(8,128)(2,1)S(1)}, bf16[256,512]{1,0:T(8,128)(2,1)}, u32[]{:S(2)}) copy-start(bf16[256,512]{1,0:T(8,128)(2,1)} %copy.224) | copy-start | bytes 786436
  115.2 1.9 %copy-start.22 = (bf16[256,512]{1,0:T(8,128)(2,1)S(1)}, bf16[256,512]{1,0:T(8,128)(2,1)}, u32[]{:S(2)}) copy-start(bf16[256,512]{1,0:T(8,128)(2,1)} %copy.221) | copy-start | bytes 786436
  115.2 1.9 %copy-start.23 = (bf16[256,512]{1,0:T(8,128)(2,1)S(1)}, bf16[256,512]{1,0:T(8,128)(2,1)}, u32[]{:S(2)}) copy-start(bf16[256,512]{1,0:T(8,128)(2,1)} %copy.223) | copy-start | bytes 786436
  115.2 1.9 %copy-start.24 = (bf16[256,512]{1,0:T(8,128)(2,1)S(1)}, bf16[256,512]{1,0:T(8,128)(2,1)}, u32[]{:S(2)}) copy-start(bf16[256,512]{1,0:T(8,128)(2,1)} %copy.222) | copy-start | bytes 786436
  117.1 39.1 %copy-start.25 = (bf16[1,1,256,1024]{2,3,1,0:T(8,128)(2,1)S(1)}, bf16[1,1,256,1024]{2,3,1,0:T(8,128)(2,1)}, u32[]{:S(2)}) copy-start(bf16[1,1,256,1024]{2,3,1,0:T(8,128)(2,1)} %fusion.85) | copy-start | bytes 1572868
  118.2 38.0 %copy-start.16 = (bf16[256,512]{0,1:T(8,128)(2,1)S(1)}, bf16[256,512]{0,1:T(8,128)(2,1)}, u32[]{:S(2)}) copy-start(bf16[256,512]{0,1:T(8,128)(2,1)} %get-tuple-element.18) | copy-start | bytes 786436
  118.2 56.2 %copy-start.6 = (bf16[4,256,256]{1,2,0:T(8,128)(2,1)S(1)}, bf16[4,256,256]{1,2,0:T(8,128)(2,1)}, u32[]{:S(2)}) copy-start(bf16[4,256,256]{1,2,0:T(8,128)(2,1)} %copy-done.5) | copy-start | bytes 1572868
  118.2 56.3 %copy-start.14 = (bf16[256,512]{0,1:T(8,128)(2,1)S(1)}, bf16[256,512]{0,1:T(8,128)(2,1)}, u32[]{:S(2)}) copy-start(bf16[256,512]{0,1:T(8,128)(2,1)} %get-tuple-element.17) | copy-start | bytes 786436
  146.1 26.0 %collective-permute-start.11 = (bf16[16,1024]{0,1:T(8,128)(2,1)S(1)}, bf16[16,1024]{0,1:T(8,128)(2,1)S(1)}, u32[]{:S(2)}, u32[]{:S(2)}) collective-permute-start(bf16[16,1024]{0,1:T(8,128)(2,1)S(1)} %convert_element_type.162), channel_id=1, source_target_pairs={{0,3},{1,4},{2,5},{3,6},{4,7},{5,8},{6,9},{7,10},{8,11},{9,12},{10... | collective-permute-start | bytes 98312 | tf_op jit(solution)/shard_map/ppermute | solution.py:19
  156.5 19.3 %collective-permute-start.10 = (bf16[16,1024]{0,1:T(8,128)(2,1)S(1)}, bf16[16,1024]{0,1:T(8,128)(2,1)S(1)}, u32[]{:S(2)}, u32[]{:S(2)}) collective-permute-start(bf16[16,1024]{0,1:T(8,128)(2,1)S(1)} %convert_element_type.162), channel_id=1, source_target_pairs={{0,61},{1,62},{2,63},{3,0},{4,1},{5,2},{6,3},{7,4},{8,5},{9,6},{10... | collective-permute-start | bytes 98312 | tf_op jit(solution)/shard_map/ppermute | solution.py:19
  161.5 14.3 %collective-permute-start.9 = (bf16[16,1024]{0,1:T(8,128)(2,1)S(1)}, bf16[16,1024]{0,1:T(8,128)(2,1)S(1)}, u32[]{:S(2)}, u32[]{:S(2)}) collective-permute-start(bf16[16,1024]{0,1:T(8,128)(2,1)S(1)} %convert_element_type.162), channel_id=1, source_target_pairs={{0,2},{1,3},{2,4},{3,5},{4,6},{5,7},{6,8},{7,9},{8,10},{9,11},{10,... | collective-permute-start | bytes 98312 | tf_op jit(solution)/shard_map/ppermute | solution.py:19
  163.4 12.4 %collective-permute-start.8 = (bf16[16,1024]{0,1:T(8,128)(2,1)S(1)}, bf16[16,1024]{0,1:T(8,128)(2,1)S(1)}, u32[]{:S(2)}, u32[]{:S(2)}) collective-permute-start(bf16[16,1024]{0,1:T(8,128)(2,1)S(1)} %convert_element_type.162), channel_id=1, source_target_pairs={{0,62},{1,63},{2,0},{3,1},{4,2},{5,3},{6,4},{7,5},{8,6},{9,7},{10,... | collective-permute-start | bytes 98312 | tf_op jit(solution)/shard_map/ppermute | solution.py:19
  170.1 5.8 %collective-permute-start.7 = (bf16[16,1024]{0,1:T(8,128)(2,1)S(1)}, bf16[16,1024]{0,1:T(8,128)(2,1)S(1)}, u32[]{:S(2)}, u32[]{:S(2)}) collective-permute-start(bf16[16,1024]{0,1:T(8,128)(2,1)S(1)} %convert_element_type.162), channel_id=1, source_target_pairs={{0,1},{1,2},{2,3},{3,4},{4,5},{5,6},{6,7},{7,8},{8,9},{9,10},{10,1... | collective-permute-start | bytes 98312 | tf_op jit(solution)/shard_map/ppermute | solution.py:19
  172.1 8.0 %collective-permute-start.6 = (bf16[16,1024]{0,1:T(8,128)(2,1)S(1)}, bf16[16,1024]{0,1:T(8,128)(2,1)}, u32[]{:S(2)}, u32[]{:S(2)}) collective-permute-start(bf16[16,1024]{0,1:T(8,128)(2,1)S(1)} %convert_element_type.162), channel_id=1, source_target_pairs={{0,63},{1,0},{2,1},{3,2},{4,3},{5,4},{6,5},{7,6},{8,7},{9,8},{10,9... | collective-permute-start | bytes 98312 | tf_op jit(solution)/shard_map/ppermute | solution.py:19
  (9 other events, 8.7 us)
Sparse Core Ops, SparseCore 0:
  108.9 36.0 reduce-scatter.3
where the time goes:
time: 193 us; the launch traced here: 189 us
  starting transfers between devices  62.8 us (33%)
  waiting for transfers between devices  30.3 us (16%)
  matrix products  28.2 us (15%)
  blocking collectives  23.1 us (12%)
  between operations  20.5 us (11%)
  local copies, waits for them, and re-layouts  18.7 us (10%)
  other arithmetic  5.41 us (3%)
    ppermute x12, starting transfers between devices, from_behind(): return lax.ppermute(value, axis, pairs)  62.8 us
    unnamed x2, waiting for transfers between devices  26.8 us
    all_gather x1, blocking collectives, shards(): full_rows = lax.all_gather(own_rows, 'prompt', axis=0, tiled=True)  23.1 us
    unnamed x62, local copies, waits for them, and re-layouts  11.7 us
    dot_general x4, matrix products, shards(): jnp.einsum('xjc,bc->jxb', query_head_block, response_key_block, preferred...  4.9 us
    reshape x4, local copies, waits for them, and re-layouts, shards(): (query_head_grad * softmax_scale).astype(jnp.bfloat16)  4.45 us
  transfers between devices with their start and end apart: 13, of which 3 were waited for; matrix products, arithmetic and copies ran while one was open for 11% of the time, Pallas kernels for 0%

commit v1 on v0

v1 whole, which is shorter than its diff:
```python
import functools
import math

import jax
import jax.numpy as jnp
from jax import lax
from jax.experimental import pallas as pl
from jax.experimental.pallas import tpu as pltpu
from jax.sharding import PartitionSpec as P

QH = 16
KVH = 4
GROUPS = QH // KVH
HD = 128
BLOCK = 128
REACH = 3
RLEN = 256
PLEN = 128
KVW = KVH * HD
QW = QH * HD
HALF = GROUPS * BLOCK
LANES = 2 * HALF
SCALE = HD**-0.5
LOG_SCALE = SCALE * math.log2(math.e)
STRIDES = (-3, 3, -2, 2, -1, 1)
MESH = pl.DeviceIdType.MESH
F32 = jnp.float32
BF16 = jnp.bfloat16
LOWEST = -3.0e38


def dot_t(a, b):
    return lax.dot_general(a, b, (((1,), (1,)), ((), ())), preferred_element_type=F32)


def dot_n(a, b):
    return lax.dot_general(a, b, (((1,), (0,)), ((), ())), preferred_element_type=F32)


def dot_l(a, b):
    return lax.dot_general(a, b, (((0,), (0,)), ((), ())), preferred_element_type=F32)


def head_rows(ref, head):
    parts = []
    for half in range(2):
        for group in range(GROUPS):
            columns = pl.ds(pl.multiple_of(head * HALF, HALF) + group * HD, HD)
            parts.append(ref[pl.ds(half * BLOCK, BLOCK), columns])
    return jnp.concatenate(parts, axis=0)


def columns_of(head, first):
    return pl.ds(pl.multiple_of(head * HD, HD) + first, HD)


def kernel(
    lengths_ref,
    owner_ref,
    q_hbm,
    kv_hbm,
    g_hbm,
    pkv_hbm,
    qg_hbm,
    rg_hbm,
    pg_hbm,
    q_ref,
    kv_ref,
    g_ref,
    land,
    gath,
    prob_resp,
    back_resp,
    stats,
    sg_prompt,
    grads,
    sums_in,
    sum_out,
    sum_land,
    qg_ref,
    rg_ref,
    pg_ref,
    in_sem,
    out_sem,
    own_sem,
    s1,
    r1,
    s2,
    r2,
    s3,
    r3,
    s4,
    r4,
):
    row = lax.axis_index("prompt")
    column = lax.axis_index("resp")
    n_row = lax.axis_size("prompt")
    n_col = lax.axis_size("resp")

    def beside(stride):
        return (row, lax.rem(column + stride + n_col, n_col))

    def above(step):
        return (lax.rem(row + step, n_row), column)

    loads = []
    for index, (source, target) in enumerate(((kv_hbm, kv_ref), (q_hbm, q_ref), (g_hbm, g_ref))):
        loads.append(pltpu.make_async_copy(source.at[0, 0], target, in_sem.at[index]))
    own = pltpu.make_async_copy(pkv_hbm.at[0], land.at[REACH], own_sem)

    barrier = pltpu.get_barrier_semaphore()
    for stride in STRIDES:
        pl.semaphore_signal(barrier, inc=1, device_id=beside(stride), device_id_type=MESH)
    for step in range(1, n_row):
        pl.semaphore_signal(barrier, inc=1, device_id=above(step), device_id_type=MESH)
    for load in loads:
        load.start()
    own.start()
    pl.semaphore_wait(barrier, len(STRIDES) + n_row - 1)

    to_readers = []
    for index, stride in enumerate(STRIDES):
        to_readers.append(
            pltpu.make_async_remote_copy(
                src_ref=pkv_hbm.at[0],
                dst_ref=land.at[REACH + stride],
                send_sem=s1.at[index],
                recv_sem=r1.at[index],
                device_id=beside(stride),
                device_id_type=MESH,
            )
        )
    for copy in to_readers:
        copy.start()

    blocks = lengths_ref[0, 0]
    key_at = lax.broadcasted_iota(jnp.int32, (BLOCK, HALF), 0)
    lane_at = lax.broadcasted_iota(jnp.int32, (BLOCK, HALF), 1)
    seen = key_at <= lax.rem(lane_at, BLOCK)

    def response(head, carry):
        span = pl.ds(pl.multiple_of(head * HALF, HALF), HALF)
        high = g_ref[pl.ds(BLOCK, BLOCK), span]
        g_ref[pl.ds(BLOCK, BLOCK), span] = jnp.where(blocks > 1, high, jnp.zeros_like(high))
        queries = head_rows(q_ref, head)
        out_grads = head_rows(g_ref, head)
        keys = kv_ref[:, columns_of(head, 0)]
        values = kv_ref[:, columns_of(head, KVW)]
        score0 = dot_t(keys[:BLOCK], queries)
        score1 = dot_t(keys[BLOCK:], queries[HALF:])
        low = jnp.where(seen, score0[:, :HALF], LOWEST)
        high0 = score0[:, HALF:]
        high1 = jnp.where(seen, score1, LOWEST)
        top_low = jnp.max(low, axis=0, keepdims=True) * LOG_SCALE
        top_high = (
            jnp.maximum(jnp.max(high0, axis=0, keepdims=True), jnp.max(high1, axis=0, keepdims=True))
            * LOG_SCALE
        )
        low = jnp.exp2(low * LOG_SCALE - top_low)
        high0 = jnp.exp2(high0 * LOG_SCALE - top_high)
        high1 = jnp.exp2(high1 * LOG_SCALE - top_high)
        mass_low = jnp.sum(low, axis=0, keepdims=True)
        mass_high = jnp.sum(high0, axis=0, keepdims=True) + jnp.sum(high1, axis=0, keepdims=True)
        low = low * (1.0 / mass_low)
        inverse = 1.0 / mass_high
        high0 = high0 * inverse
        high1 = high1 * inverse
        back0 = dot_t(values[:BLOCK], out_grads)
        back1 = dot_t(values[BLOCK:], out_grads[HALF:])
        delta_low = jnp.sum(low * back0[:, :HALF], axis=0, keepdims=True)
        delta_high = jnp.sum(high0 * back0[:, HALF:], axis=0, keepdims=True) + jnp.sum(
            high1 * back1, axis=0, keepdims=True
        )
        prob_resp[head, 0] = low
        prob_resp[head, 1] = high0
        prob_resp[head, 2] = high1
        back_resp[head, 0] = back0[:, :HALF]
        back_resp[head, 1] = back0[:, HALF:]
        back_resp[head, 2] = back1
        stats[head, 0:1] = jnp.concatenate([top_low, top_high], axis=1)
        stats[head, 1:2] = jnp.concatenate([mass_low, mass_high], axis=1)
        stats[head, 2:3] = jnp.concatenate([delta_low, delta_high], axis=1)
        return carry

    for load in loads:
        load.wait()
    lax.fori_loop(0, KVH // 2, response, 0)

    own.wait()
    for copy in to_readers:
        copy.wait()
    wanted = owner_ref[column]
    offset = lax.rem(column - wanted + n_col + REACH, n_col)
    mine = pl.ds(pl.multiple_of(row * 16, 16), 16)
    gath[mine] = land[jnp.minimum(offset, 2 * REACH)]
    spread = []
    for part in range(2):
        for step in (4, 3, 5, 2, 6, 1, 7):
            block = gath.at[mine, pl.ds(part * KVW, KVW)]
            spread.append(
                pltpu.make_async_remote_copy(
                    src_ref=block,
                    dst_ref=block,
                    send_sem=s2.at[part, step],
                    recv_sem=r2.at[part, step],
                    device_id=above(step),
                    device_id_type=MESH,
                )
            )
    for copy in spread:
        copy.start()
    lax.fori_loop(KVH // 2, KVH, response, 0)
    for copy in spread:
        copy.wait()

    def to_row(head, step):
        target = lax.rem(row + step, n_row)
        return pltpu.make_async_remote_copy(
            src_ref=grads.at[head, pl.ds(pl.multiple_of(target * 16, 16), 16)],
            dst_ref=sums_in.at[step, head],
            send_sem=s3.at[step],
            recv_sem=r3.at[step],
            device_id=above(step),
            device_id_type=MESH,
        )

    def prompt(head, carry):
        queries = head_rows(q_ref, head)
        out_grads = head_rows(g_ref, head)
        keys = gath[:, columns_of(head, 0)]
        values = gath[:, columns_of(head, KVW)]
        score = dot_t(keys, queries)
        top_resp = stats[head, 0:1]
        top = jnp.maximum(jnp.max(score, axis=0, keepdims=True) * LOG_SCALE, top_resp)
        prob = jnp.exp2(score * LOG_SCALE - top)
        mass_resp = jnp.exp2(top_resp - top) * stats[head, 1:2]
        inverse = 1.0 / (mass_resp + jnp.sum(prob, axis=0, keepdims=True))
        share = mass_resp * inverse
        prob = prob * inverse
        back = dot_t(values, out_grads)
        delta = share * stats[head, 2:3] + jnp.sum(prob * back, axis=0, keepdims=True)
        score_grad = (prob * (back - delta)).astype(BF16)
        grads[head, :, :HD] = (dot_n(score_grad, queries) * SCALE).astype(BF16)
        grads[head, :, HD:] = dot_n(prob.astype(BF16), out_grads).astype(BF16)
        sg_prompt[head] = score_grad
        stats[head, 3:4] = share
        stats[head, 4:5] = delta
        for step in (4, 3, 5, 2, 6, 1, 7):
            to_row(head, step).start()
        return carry

    lax.fori_loop(0, KVH, prompt, 0)

    def finish(head, carry):
        queries = head_rows(q_ref, head)
        out_grads = head_rows(g_ref, head)
        keys = kv_ref[:, columns_of(head, 0)]
        prompt_keys = gath[:, columns_of(head, 0)]
        share = stats[head, 3:4]
        delta = stats[head, 4:5]
        low = prob_resp[head, 0] * share[:, :HALF]
        high0 = prob_resp[head, 1] * share[:, HALF:]
        high1 = prob_resp[head, 2] * share[:, HALF:]
        sg_low = (low * (back_resp[head, 0] - delta[:, :HALF])).astype(BF16)
        sg_high0 = (high0 * (back_resp[head, 1] - delta[:, HALF:])).astype(BF16)
        sg_high1 = (high1 * (back_resp[head, 2] - delta[:, HALF:])).astype(BF16)
        sg0 = jnp.concatenate([sg_low, sg_high0], axis=1)
        pr0 = jnp.concatenate([low.astype(BF16), high0.astype(BF16)], axis=1)
        key_at = columns_of(head, 0)
        value_at = columns_of(head, KVW)
        rg_ref[pl.ds(0, BLOCK), key_at] = (dot_n(sg0, queries) * SCALE).astype(BF16)
        rg_ref[pl.ds(BLOCK, BLOCK), key_at] = (dot_n(sg_high1, queries[HALF:]) * SCALE).astype(BF16)
        rg_ref[pl.ds(0, BLOCK), value_at] = dot_n(pr0, out_grads).astype(BF16)
        rg_ref[pl.ds(BLOCK, BLOCK), value_at] = dot_n(high1.astype(BF16), out_grads[HALF:]).astype(BF16)
        sgp = sg_prompt[head]
        grad_low = dot_l(
            jnp.concatenate([sgp[:, :HALF], sg_low], axis=0),
            jnp.concatenate([prompt_keys, keys[:BLOCK]], axis=0),
        )
        grad_high = dot_l(
            jnp.concatenate([sgp[:, HALF:], sg_high0, sg_high1], axis=0),
            jnp.concatenate([prompt_keys, keys], axis=0),
        )
        for half, grad in enumerate((grad_low, grad_high)):
            grad = (grad * SCALE).astype(BF16)
            for group in range(GROUPS):
                at = pl.ds(pl.multiple_of(head * HALF, HALF) + group * HD, HD)
                qg_ref[pl.ds(half * BLOCK, BLOCK), at] = grad[group * BLOCK : (group + 1) * BLOCK]
        return carry

    lax.fori_loop(0, KVH, finish, 0)
    stores = [
        pltpu.make_async_copy(qg_ref, qg_hbm.at[0, 0], out_sem.at[0]),
        pltpu.make_async_copy(rg_ref, rg_hbm.at[0, 0], out_sem.at[1]),
    ]
    for store in stores:
        store.start()

    total = grads[:, mine].astype(F32)
    for step in range(1, n_row):
        pltpu.make_async_remote_copy(
            src_ref=sums_in.at[step],
            dst_ref=sums_in.at[step],
            send_sem=s3.at[step],
            recv_sem=r3.at[step],
            device_id=above(step),
            device_id_type=MESH,
        ).wait()
        total = total + sums_in[step].astype(F32)
    sum_out[...] = total.astype(BF16)
    to_owners = []
    for index, stride in enumerate(STRIDES):
        to_owners.append(
            pltpu.make_async_remote_copy(
                src_ref=sum_out,
                dst_ref=sum_land.at[index],
                send_sem=s4.at[index],
                recv_sem=r4.at[index],
                device_id=beside(stride),
                device_id_type=MESH,
            )
        )
    for copy in to_owners:
        copy.start()
    total = jnp.where(wanted == column, total, 0.0)
    for index, stride in enumerate(STRIDES):
        to_owners[index].wait()
        reads = owner_ref[lax.rem(column - stride + n_col, n_col)] == column
        total = total + jnp.where(reads, sum_land[index].astype(F32), 0.0)
    for head in range(KVH):
        pg_ref[:, head * HD : (head + 1) * HD] = total[head, :, :HD]
        pg_ref[:, KVW + head * HD : KVW + (head + 1) * HD] = total[head, :, HD:]
    store = pltpu.make_async_copy(pg_ref, pg_hbm.at[0], out_sem.at[2])
    store.start()
    stores.append(store)
    for store in stores:
        store.wait()


def shards(queries, resp_kv, out_grad, prompt_kv, prompt_of, lengths):
    any_spec = pl.BlockSpec(memory_space=pl.ANY)
    smem_spec = pl.BlockSpec(memory_space=pltpu.SMEM)
    return pl.pallas_call(
        kernel,
        out_shape=(
            jax.ShapeDtypeStruct(queries.shape, BF16),
            jax.ShapeDtypeStruct(resp_kv.shape, BF16),
            jax.ShapeDtypeStruct(prompt_kv.shape, F32),
        ),
        in_specs=[smem_spec, smem_spec] + [any_spec] * 4,
        out_specs=(any_spec,) * 3,
        scratch_shapes=[
            pltpu.VMEM((RLEN, QW), BF16),
            pltpu.VMEM((RLEN, 2 * KVW), BF16),
            pltpu.VMEM((RLEN, QW), BF16),
            pltpu.VMEM((2 * REACH + 1, 16, 2 * KVW), BF16),
            pltpu.VMEM((PLEN, 2 * KVW), BF16),
            pltpu.VMEM((KVH, 3, BLOCK, HALF), F32),
            pltpu.VMEM((KVH, 3, BLOCK, HALF), F32),
            pltpu.VMEM((KVH, 8, LANES), F32),
            pltpu.VMEM((KVH, PLEN, LANES), BF16),
            pltpu.VMEM((KVH, PLEN, 2 * HD), BF16),
            pltpu.VMEM((8, KVH, 16, 2 * HD), BF16),
            pltpu.VMEM((KVH, 16, 2 * HD), BF16),
            pltpu.VMEM((2 * REACH, KVH, 16, 2 * HD), BF16),
            pltpu.VMEM((RLEN, QW), BF16),
            pltpu.VMEM((RLEN, 2 * KVW), BF16),
            pltpu.VMEM((16, 2 * KVW), F32),
            pltpu.SemaphoreType.DMA((3,)),
            pltpu.SemaphoreType.DMA((3,)),
            pltpu.SemaphoreType.DMA,
            pltpu.SemaphoreType.DMA((6,)),
            pltpu.SemaphoreType.DMA((6,)),
            pltpu.SemaphoreType.DMA((2, 8)),
            pltpu.SemaphoreType.DMA((2, 8)),
            pltpu.SemaphoreType.DMA((8,)),
            pltpu.SemaphoreType.DMA((8,)),
            pltpu.SemaphoreType.DMA((6,)),
            pltpu.SemaphoreType.DMA((6,)),
        ],
        compiler_params=pltpu.CompilerParams(
            collective_id=0, has_side_effects=True, vmem_limit_bytes=56 << 20
        ),
        name="slot_grads",
    )(lengths, prompt_of, queries, resp_kv, out_grad, prompt_kv)


def solution(mesh):
    return jax.shard_map(
        shards,
        mesh=mesh,
        in_specs=(
            P("prompt", "resp", None, None),
            P("prompt", "resp", None, None),
            P("prompt", "resp", None, None),
            P("resp", "prompt", None),
            P(),
            P("prompt", "resp"),
        ),
        out_specs=(
            P("prompt", "resp", None, None),
            P("prompt", "resp", None, None),
            P("resp", "prompt", None),
        ),
        check_vma=False,
    )
```

time: 193 us -> 49.8 us (0.26); the launches traced: 189 us -> 49.6 us
  starting transfers between devices: 62.8 us -> 0 us
  Pallas kernels: 0 us -> 44.4 us
  waiting for transfers between devices: 30.3 us -> 0 us
  matrix products: 28.2 us -> 0 us
  blocking collectives: 23.1 us -> 0 us
  between operations: 20.5 us -> 1.3 us
  local copies, waits for them, and re-layouts: 18.7 us -> 3.86 us
  other arithmetic: 5.41 us -> 0 us
    ppermute x12 -> x0, starting transfers between devices: 62.8 us -> none  [from_behind(): return lax.ppermute(value, axis, pairs)]
    pallas_call x0 -> x1, Pallas kernels: none -> 44.4 us  [shards(): pl.pallas_call(kernel, out_shape=(jax.ShapeDtypeStruct(queries.shape, BF1...]
    dot_general x48 -> x0, matrix products: 28.2 us -> none  [the longest x4 4.9 us: shards(): jnp.einsum('xjc,bc->jxb', query_head_block, response_key_block, preferred...]
    unnamed x2 -> x0, waiting for transfers between devices: 26.8 us -> none
    all_gather x1 -> x0, blocking collectives: 23.1 us -> none  [shards(): full_rows = lax.all_gather(own_rows, 'prompt', axis=0, tiled=True)]
    unnamed x62 -> x7, local copies, waits for them, and re-layouts: 11.7 us -> 3.86 us
    reshape x4 -> x0, local copies, waits for them, and re-layouts: 4.45 us -> none  [shards(): (query_head_grad * softmax_scale).astype(jnp.bfloat16)]
    ppermute x12 -> x0, waiting for transfers between devices: 3.56 us -> none  [from_behind(): return lax.ppermute(value, axis, pairs)]
  transfers between devices with their start and end apart: 13 -> 0, of which waited for: 3 -> 0; matrix products, arithmetic and copies ran while one was open for 11% -> 0% of each run, Pallas kernels for 0% -> 0%
where the time goes in v1:
time: 49.8 us; the launch traced here: 49.6 us
  Pallas kernels  44.4 us (89%)
  local copies, waits for them, and re-layouts  3.86 us (8%)
  between operations  1.3 us (3%)
    pallas_call x1, Pallas kernels, shards(): pl.pallas_call(kernel, out_shape=(jax.ShapeDtypeStruct(queries.shape, BF1...  44.4 us
    unnamed x7, local copies, waits for them, and re-layouts  3.86 us

profile of v1, /device:TPU:1, one launch (start us, length us, event | category | flops | bytes accessed | tf_op | source)
XLA Modules:
  0.0 49.6 jit_solution(14156833130171550940)
XLA Ops:
  1.3 44.4 %slot_grads.1 = (bf16[1,1,256,2048]{3,2,1,0:T(8,128)(2,1)}, bf16[1,1,256,1024]{3,2,1,0:T(8,128)(2,1)}, f32[1,16,1024]{2,1,0:T(8,128)}) custom-call(s32[1,1]{1,0:T(1,128)S(6)} %copy.12.lengths_ref, s32[64]{0:T(128)} %owner_ref.1, bf16[1,1,256,2048]{3,2,1,0:T(8,128)(2,1)} %q_hbm.1, bf16[1,1,256,1024]{3,2,1,0:T(8,128)(2,1)} %kv_hbm.1, ...), custom_call_target="tpu_custom_call" | custom-call | tf_op jit(solution)/shard_map/slot_grads/pallas_call | solution.py:343
  45.7 0.0 copy-start
  45.7 2.4 %copy.13 = bf16[1,1,256,2048]{3,2,1,0:T(8,128)(2,1)} copy(bf16[1,1,256,2048]{3,2,1,0:T(8,128)(2,1)} %get-tuple-element.6) | data formatting | bytes 2097152
  48.1 0.0 copy-done
  48.1 0.0 copy-start.1
  48.1 0.8 %copy.14 = bf16[1,1,256,1024]{3,2,1,0:T(8,128)(2,1)} copy(bf16[1,1,256,1024]{3,2,1,0:T(8,128)(2,1)S(1)} %copy-done) | data formatting | bytes 1048576
  48.9 0.1 copy-done.1
  48.9 0.6 %copy.15 = f32[1,16,1024]{2,1,0:T(8,128)} copy(f32[1,16,1024]{2,1,0:T(8,128)S(1)} %copy-done.1) | data formatting | bytes 131072
Async XLA Ops:
  45.7 2.4 %copy-start = (bf16[1,1,256,1024]{3,2,1,0:T(8,128)(2,1)S(1)}, bf16[1,1,256,1024]{3,2,1,0:T(8,128)(2,1)}, u32[]{:S(2)}) copy-start(bf16[1,1,256,1024]{3,2,1,0:T(8,128)(2,1)} %get-tuple-element.7) | copy-start | bytes 1572868
  48.1 0.9 %copy-start.1 = (f32[1,16,1024]{2,1,0:T(8,128)S(1)}, f32[1,16,1024]{2,1,0:T(8,128)}, u32[]{:S(2)}) copy-start(f32[1,16,1024]{2,1,0:T(8,128)} %get-tuple-element.8) | copy-start | bytes 196612

commit v2 on v1

--- a/solution.py
+++ b/solution.py
@@ -22,7 +22,10 @@
 LANES = 2 * HALF
 SCALE = HD**-0.5
 LOG_SCALE = SCALE * math.log2(math.e)
+CHUNKS = 2
+PER = KVH // CHUNKS
 STRIDES = (-3, 3, -2, 2, -1, 1)
+STEPS = (4, 3, 5, 2, 6, 1, 7)
 MESH = pl.DeviceIdType.MESH
 F32 = jnp.float32
 BF16 = jnp.bfloat16
@@ -56,18 +59,21 @@
 
 def kernel(
     lengths_ref,
-    owner_ref,
+    owner_hbm,
     q_hbm,
     kv_hbm,
     g_hbm,
     pkv_hbm,
-    qg_hbm,
-    rg_hbm,
-    pg_hbm,
+    qg_ref,
+    rg_ref,
+    pg_ref,
+    owner_ref,
     q_ref,
     kv_ref,
     g_ref,
-    land,
+    own_ref,
+    land0,
+    land1,
     gath,
     prob_resp,
     back_resp,
@@ -77,12 +83,7 @@
     sums_in,
     sum_out,
     sum_land,
-    qg_ref,
-    rg_ref,
-    pg_ref,
     in_sem,
-    out_sem,
-    own_sem,
     s1,
     r1,
     s2,
@@ -92,6 +93,7 @@
     s4,
     r4,
 ):
+    land = (land0, land1)
     row = lax.axis_index("prompt")
     column = lax.axis_index("resp")
     n_row = lax.axis_size("prompt")
@@ -103,35 +105,47 @@
     def above(step):
         return (lax.rem(row + step, n_row), column)
 
-    loads = []
-    for index, (source, target) in enumerate(((kv_hbm, kv_ref), (q_hbm, q_ref), (g_hbm, g_ref))):
-        loads.append(pltpu.make_async_copy(source.at[0, 0], target, in_sem.at[index]))
-    own = pltpu.make_async_copy(pkv_hbm.at[0], land.at[REACH], own_sem)
-
+    def heads_of(chunk):
+        return pl.ds(chunk * PER, PER)
+
+    own = pltpu.make_async_copy(pkv_hbm.at[0], own_ref, in_sem.at[0])
+    own.start()
     barrier = pltpu.get_barrier_semaphore()
     for stride in STRIDES:
         pl.semaphore_signal(barrier, inc=1, device_id=beside(stride), device_id_type=MESH)
-    for step in range(1, n_row):
+    for step in STEPS:
         pl.semaphore_signal(barrier, inc=1, device_id=above(step), device_id_type=MESH)
+    loads = []
+    for source, target in (
+        (owner_hbm, owner_ref),
+        (kv_hbm.at[0, 0], kv_ref),
+        (q_hbm.at[0, 0], q_ref),
+        (g_hbm.at[0, 0], g_ref),
+    ):
+        loads.append(pltpu.make_async_copy(source, target, in_sem.at[len(loads) + 1]))
+        loads[-1].start()
+    own.wait()
+    for head in range(KVH):
+        part = land[head // PER].at[REACH, head % PER]
+        part[:, :HD] = own_ref[:, head * HD : (head + 1) * HD]
+        part[:, HD:] = own_ref[:, KVW + head * HD : KVW + (head + 1) * HD]
+    pl.semaphore_wait(barrier, len(STRIDES) + n_row - 1)
+
+    def to_reader(chunk, index):
+        return pltpu.make_async_remote_copy(
+            src_ref=land[chunk].at[REACH],
+            dst_ref=land[chunk].at[REACH + STRIDES[index]],
+            send_sem=s1.at[chunk, index],
+            recv_sem=r1.at[chunk, index],
+            device_id=beside(STRIDES[index]),
+            device_id_type=MESH,
+        )
+
+    for chunk in range(CHUNKS):
+        for index in range(len(STRIDES)):
+            to_reader(chunk, index).start()
     for load in loads:
-        load.start()
-    own.start()
-    pl.semaphore_wait(barrier, len(STRIDES) + n_row - 1)
-
-    to_readers = []
-    for index, stride in enumerate(STRIDES):
-        to_readers.append(
-            pltpu.make_async_remote_copy(
-                src_ref=pkv_hbm.at[0],
-                dst_ref=land.at[REACH + stride],
-                send_sem=s1.at[index],
-                recv_sem=r1.at[index],
-                device_id=beside(stride),
-                device_id_type=MESH,
-            )
-        )
-    for copy in to_readers:
-        copy.start()
+        load.wait()
 
     blocks = lengths_ref[0, 0]
     key_at = lax.broadcasted_iota(jnp.int32, (BLOCK, HALF), 0)
@@ -182,44 +196,37 @@
         stats[head, 2:3] = jnp.concatenate([delta_low, delta_high], axis=1)
         return carry
 
-    for load in loads:
-        load.wait()
-    lax.fori_loop(0, KVH // 2, response, 0)
-
-    own.wait()
-    for copy in to_readers:
-        copy.wait()
+    lax.fori_loop(0, KVH, response, 0)
+
     wanted = owner_ref[column]
-    offset = lax.rem(column - wanted + n_col + REACH, n_col)
+    offset = jnp.minimum(lax.rem(column - wanted + n_col + REACH, n_col), 2 * REACH)
     mine = pl.ds(pl.multiple_of(row * 16, 16), 16)
-    gath[mine] = land[jnp.minimum(offset, 2 * REACH)]
-    spread = []
-    for part in range(2):
-        for step in (4, 3, 5, 2, 6, 1, 7):
-            block = gath.at[mine, pl.ds(part * KVW, KVW)]
-            spread.append(
-                pltpu.make_async_remote_copy(
-                    src_ref=block,
-                    dst_ref=block,
-                    send_sem=s2.at[part, step],
-                    recv_sem=r2.at[part, step],
-                    device_id=above(step),
-                    device_id_type=MESH,
-                )
-            )
-    for copy in spread:
-        copy.start()
-    lax.fori_loop(KVH // 2, KVH, response, 0)
-    for copy in spread:
-        copy.wait()
-
-    def to_row(head, step):
+
+    def along(chunk, step):
+        block = gath.at[heads_of(chunk), mine]
+        return pltpu.make_async_remote_copy(
+            src_ref=block,
+            dst_ref=block,
+            send_sem=s2.at[chunk, step],
+            recv_sem=r2.at[chunk, step],
+            device_id=above(step),
+            device_id_type=MESH,
+        )
+
+    for chunk in range(CHUNKS):
+        for index in range(len(STRIDES)):
+            to_reader(chunk, index).wait_recv()
+        gath[heads_of(chunk), mine] = land[chunk][offset]
+        for step in STEPS:
+            along(chunk, step).start()
+
+    def to_row(chunk, step):
         target = lax.rem(row + step, n_row)
         return pltpu.make_async_remote_copy(
-            src_ref=grads.at[head, pl.ds(pl.multiple_of(target * 16, 16), 16)],
-            dst_ref=sums_in.at[step, head],
-            send_sem=s3.at[step],
-            recv_sem=r3.at[step],
+            src_ref=grads.at[heads_of(chunk), pl.ds(pl.multiple_of(target * 16, 16), 16)],
+            dst_ref=sums_in.at[step, heads_of(chunk)],
+            send_sem=s3.at[chunk, step],
+            recv_sem=r3.at[chunk, step],
             device_id=above(step),
             device_id_type=MESH,
         )
@@ -227,8 +234,8 @@
     def prompt(head, carry):
         queries = head_rows(q_ref, head)
         out_grads = head_rows(g_ref, head)
-        keys = gath[:, columns_of(head, 0)]
-        values = gath[:, columns_of(head, KVW)]
+        keys = gath[head, :, :HD]
+        values = gath[head, :, HD:]
         score = dot_t(keys, queries)
         top_resp = stats[head, 0:1]
         top = jnp.maximum(jnp.max(score, axis=0, keepdims=True) * LOG_SCALE, top_resp)
@@ -245,17 +252,20 @@
         sg_prompt[head] = score_grad
         stats[head, 3:4] = share
         stats[head, 4:5] = delta
-        for step in (4, 3, 5, 2, 6, 1, 7):
-            to_row(head, step).start()
         return carry
 
-    lax.fori_loop(0, KVH, prompt, 0)
+    for chunk in range(CHUNKS):
+        for step in STEPS:
+            along(chunk, step).wait_recv()
+        lax.fori_loop(chunk * PER, (chunk + 1) * PER, prompt, 0)
+        for step in STEPS:
+            to_row(chunk, step).start()
 
     def finish(head, carry):
         queries = head_rows(q_ref, head)
         out_grads = head_rows(g_ref, head)
         keys = kv_ref[:, columns_of(head, 0)]
-        prompt_keys = gath[:, columns_of(head, 0)]
+        prompt_keys = gath[head, :, :HD]
         share = stats[head, 3:4]
         delta = stats[head, 4:5]
         low = prob_resp[head, 0] * share[:, :HALF]
@@ -289,72 +299,82 @@
         return carry
 
     lax.fori_loop(0, KVH, finish, 0)
+
+    def to_owner(chunk, index):
+        return pltpu.make_async_remote_copy(
+            src_ref=sum_out.at[heads_of(chunk)],
+            dst_ref=sum_land.at[index, heads_of(chunk)],
+            send_sem=s4.at[chunk, index],
+            recv_sem=r4.at[chunk, index],
+            device_id=beside(STRIDES[index]),
+            device_id_type=MESH,
+        )
+
+    totals = []
+    for chunk in range(CHUNKS):
+        total = grads[heads_of(chunk), mine].astype(F32)
+        for step in STEPS:
+            to_row(chunk, step).wait_recv()
+        for step in STEPS:
+            total = total + sums_in[step, heads_of(chunk)].astype(F32)
+        sum_out[heads_of(chunk)] = total.astype(BF16)
+        for index in range(len(STRIDES)):
+            to_owner(chunk, index).start()
+        totals.append(jnp.where(wanted == column, total, 0.0))
+    for chunk in range(CHUNKS):
+        for index in range(len(STRIDES)):
+            to_reader(chunk, index).wait_send()
+        for step in STEPS:
+            along(chunk, step).wait_send()
+            to_row(chunk, step).wait_send()
+    for chunk in range(CHUNKS):
+        total = totals[chunk]
+        for index in range(len(STRIDES)):
+            to_owner(chunk, index).wait()
+        for index, stride in enumerate(STRIDES):
+            reads = owner_ref[lax.rem(column - stride + n_col, n_col)] == column
+            total = total + jnp.where(reads, sum_land[index, heads_of(chunk)].astype(F32), 0.0)
+        for at in range(PER):
+            head = chunk * PER + at
+            pg_ref[:, head * HD : (head + 1) * HD] = total[at, :, :HD]
+            pg_ref[:, KVW + head * HD : KVW + (head + 1) * HD] = total[at, :, HD:]
+
+
+def store_kernel(qg_ref, rg_ref, pg_ref, qg_hbm, rg_hbm, pg_hbm, sem):
     stores = [
-        pltpu.make_async_copy(qg_ref, qg_hbm.at[0, 0], out_sem.at[0]),
-        pltpu.make_async_copy(rg_ref, rg_hbm.at[0, 0], out_sem.at[1]),
+        pltpu.make_async_copy(qg_ref, qg_hbm.at[0, 0], sem.at[0]),
+        pltpu.make_async_copy(rg_ref, rg_hbm.at[0, 0], sem.at[1]),
+        pltpu.make_async_copy(pg_ref, pg_hbm.at[0], sem.at[2]),
     ]
     for store in stores:
         store.start()
-
-    total = grads[:, mine].astype(F32)
-    for step in range(1, n_row):
-        pltpu.make_async_remote_copy(
-            src_ref=sums_in.at[step],
-            dst_ref=sums_in.at[step],
-            send_sem=s3.at[step],
-            recv_sem=r3.at[step],
-            device_id=above(step),
-            device_id_type=MESH,
-        ).wait()
-        total = total + sums_in[step].astype(F32)
-    sum_out[...] = total.astype(BF16)
-    to_owners = []
-    for index, stride in enumerate(STRIDES):
-        to_owners.append(
-            pltpu.make_async_remote_copy(
-                src_ref=sum_out,
-                dst_ref=sum_land.at[index],
-                send_sem=s4.at[index],
-                recv_sem=r4.at[index],
-                device_id=beside(stride),
-                device_id_type=MESH,
-            )
-        )
-    for copy in to_owners:
-        copy.start()
-    total = jnp.where(wanted == column, total, 0.0)
-    for index, stride in enumerate(STRIDES):
-        to_owners[index].wait()
-        reads = owner_ref[lax.rem(column - stride + n_col, n_col)] == column
-        total = total + jnp.where(reads, sum_land[index].astype(F32), 0.0)
-    for head in range(KVH):
-        pg_ref[:, head * HD : (head + 1) * HD] = total[head, :, :HD]
-        pg_ref[:, KVW + head * HD : KVW + (head + 1) * HD] = total[head, :, HD:]
-    store = pltpu.make_async_copy(pg_ref, pg_hbm.at[0], out_sem.at[2])
-    store.start()
-    stores.append(store)
     for store in stores:
         store.wait()
 
 
 def shards(queries, resp_kv, out_grad, prompt_kv, prompt_of, lengths):
-    any_spec = pl.BlockSpec(memory_space=pl.ANY)
-    smem_spec = pl.BlockSpec(memory_space=pltpu.SMEM)
-    return pl.pallas_call(
+    in_hbm = pl.BlockSpec(memory_space=pltpu.HBM)
+    in_vmem = pl.BlockSpec(memory_space=pltpu.VMEM)
+    operands = (lengths, prompt_of, queries, resp_kv, out_grad, prompt_kv)
+    operands = (pltpu.with_memory_space_constraint(lengths, pltpu.SMEM),) + tuple(pltpu.with_memory_space_constraint(operand, pltpu.HBM) for operand in operands[1:])
+    results = pl.pallas_call(
         kernel,
         out_shape=(
-            jax.ShapeDtypeStruct(queries.shape, BF16),
-            jax.ShapeDtypeStruct(resp_kv.shape, BF16),
-            jax.ShapeDtypeStruct(prompt_kv.shape, F32),
+            pltpu.VMEM((RLEN, QW), BF16),
+            pltpu.VMEM((RLEN, 2 * KVW), BF16),
+            pltpu.VMEM((16, 2 * KVW), F32),
         ),
-        in_specs=[smem_spec, smem_spec] + [any_spec] * 4,
-        out_specs=(any_spec,) * 3,
+        in_specs=[pl.BlockSpec(memory_space=pltpu.SMEM)] + [in_hbm] * 5,
+        out_specs=(in_vmem,) * 3,
         scratch_shapes=[
+            pltpu.SMEM((64,), jnp.int32),
             pltpu.VMEM((RLEN, QW), BF16),
             pltpu.VMEM((RLEN, 2 * KVW), BF16),
             pltpu.VMEM((RLEN, QW), BF16),
-            pltpu.VMEM((2 * REACH + 1, 16, 2 * KVW), BF16),
-            pltpu.VMEM((PLEN, 2 * KVW), BF16),
+            pltpu.VMEM((16, 2 * KVW), BF16),
+            pltpu.VMEM((2 * REACH + 1, PER, 16, 2 * HD), BF16),
+            pltpu.VMEM((2 * REACH + 1, PER, 16, 2 * HD), BF16),
+            pltpu.VMEM((KVH, PLEN, 2 * HD), BF16),
             pltpu.VMEM((KVH, 3, BLOCK, HALF), F32),
             pltpu.VMEM((KVH, 3, BLOCK, HALF), F32),
             pltpu.VMEM((KVH, 8, LANES), F32),
@@ -363,26 +383,34 @@
             pltpu.VMEM((8, KVH, 16, 2 * HD), BF16),
             pltpu.VMEM((KVH, 16, 2 * HD), BF16),
             pltpu.VMEM((2 * REACH, KVH, 16, 2 * HD), BF16),
-            pltpu.VMEM((RLEN, QW), BF16),
-            pltpu.VMEM((RLEN, 2 * KVW), BF16),
-            pltpu.VMEM((16, 2 * KVW), F32),
-            pltpu.SemaphoreType.DMA((3,)),
-            pltpu.SemaphoreType.DMA((3,)),
-            pltpu.SemaphoreType.DMA,
             pltpu.SemaphoreType.DMA((6,)),
-            pltpu.SemaphoreType.DMA((6,)),
-            pltpu.SemaphoreType.DMA((2, 8)),
-            pltpu.SemaphoreType.DMA((2, 8)),
-            pltpu.SemaphoreType.DMA((8,)),
-            pltpu.SemaphoreType.DMA((8,)),
-            pltpu.SemaphoreType.DMA((6,)),
-            pltpu.SemaphoreType.DMA((6,)),
+            pltpu.SemaphoreType.DMA((CHUNKS, 6)),
+            pltpu.SemaphoreType.DMA((CHUNKS, 6)),
+            pltpu.SemaphoreType.DMA((CHUNKS, 8)),
+            pltpu.SemaphoreType.DMA((CHUNKS, 8)),
+            pltpu.SemaphoreType.DMA((CHUNKS, 8)),
+            pltpu.SemaphoreType.DMA((CHUNKS, 8)),
+            pltpu.SemaphoreType.DMA((CHUNKS, 6)),
+            pltpu.SemaphoreType.DMA((CHUNKS, 6)),
         ],
         compiler_params=pltpu.CompilerParams(
-            collective_id=0, has_side_effects=True, vmem_limit_bytes=56 << 20
+            collective_id=0, has_side_effects=True, vmem_limit_bytes=40 << 20
         ),
         name="slot_grads",
-    )(lengths, prompt_of, queries, resp_kv, out_grad, prompt_kv)
+    )(*operands)
+    results = [pltpu.with_memory_space_constraint(result, pltpu.VMEM) for result in results]
+    return pl.pallas_call(
+        store_kernel,
+        out_shape=(
+            jax.ShapeDtypeStruct(queries.shape, BF16),
+            jax.ShapeDtypeStruct(resp_kv.shape, BF16),
+            jax.ShapeDtypeStruct(prompt_kv.shape, F32),
+        ),
+        in_specs=[in_vmem] * 3,
+        out_specs=(in_hbm,) * 3,
+        scratch_shapes=[pltpu.SemaphoreType.DMA((3,))],
+        name="store",
+    )(*results)
 
 
 def solution(mesh):

time: 49.8 us -> 43.3 us (0.87)
  local copies, waits for them, and re-layouts: 3.86 us -> 0 us
  Pallas kernels: 44.4 us -> 41.9 us
    unnamed x7 -> x0, local copies, waits for them, and re-layouts: 3.86 us -> none
    pallas_call x1 -> x2, Pallas kernels: 44.4 us -> 41.9 us  [the longest x1 40.7 us: shards(): pl.pallas_call(kernel, out_shape=(pltpu.VMEM((RLEN, QW), BF16), pltpu.VME...]
where the time goes in v2:
time: 43.3 us; the launch traced here: 43.2 us
  Pallas kernels  41.9 us (97%)
  between operations  1.29 us (3%)
    pallas_call x1, Pallas kernels, shards(): pl.pallas_call(kernel, out_shape=(pltpu.VMEM((RLEN, QW), BF16), pltpu.VME...  40.7 us
    pallas_call x1, Pallas kernels, shards(): pl.pallas_call(store_kernel, out_shape=(jax.ShapeDtypeStruct(queries.shap...  1.18 us

profile of v2, /device:TPU:1, one launch (start us, length us, event | category | flops | bytes accessed | tf_op | source)
XLA Modules:
  0.0 43.2 jit_solution(17033624535576543619)
XLA Ops:
  1.3 40.7 %slot_grads.1 = (bf16[256,2048]{1,0:T(8,128)(2,1)S(1)}, bf16[256,1024]{1,0:T(8,128)(2,1)S(1)}, f32[16,1024]{1,0:T(8,128)S(1)}) custom-call(s32[1,1]{1,0:T(1,128)S(6)} %copy.9.lengths_ref, s32[64]{0:T(128)} %owner_hbm.1, bf16[1,1,256,2048]{3,2,1,0:T(8,128)(2,1)} %q_hbm.1, bf16[1,1,256,1024]{3,2,1,0:T(8,128)(2,1)} %kv_hbm.1, bf16[1,1,256,2048]{3,2,1,0:T(8,128)(2,1)} %g_hbm.1, ...), custom_call_target="tpu_custom_call" | custom-call | tf_op jit(solution)/shard_map/slot_grads/pallas_call | solution.py:360
  42.0 1.2 %store.1 = (bf16[1,1,256,2048]{3,2,1,0:T(8,128)(2,1)}, bf16[1,1,256,1024]{3,2,1,0:T(8,128)(2,1)}, f32[1,16,1024]{2,1,0:T(8,128)}) custom-call(bf16[256,2048]{1,0:T(8,128)(2,1)S(1)} %get-tuple-element.6.qg_ref, bf16[256,1024]{1,0:T(8,128)(2,1)S(1)} %get-tuple-element.7.rg_ref, f32[16,1024]{1,0:T(8,128)S(1)} %get-tuple-element.8.pg_ref), custom_call_target="tpu_custom_call" | custom-call | tf_op jit(solution)/shard_map/store/pallas_call | solution.py:402

commit v3 on v2

--- a/solution.py
+++ b/solution.py
@@ -22,10 +22,12 @@
 LANES = 2 * HALF
 SCALE = HD**-0.5
 LOG_SCALE = SCALE * math.log2(math.e)
-CHUNKS = 2
-PER = KVH // CHUNKS
+PROMPT_PARTS = ((0, 2), (2, 1), (3, 1))
+GRAD_PARTS = ((0, 1), (1, 1), (2, 1), (3, 1))
+SUM_PARTS = ((0, 2), (2, 2))
 STRIDES = (-3, 3, -2, 2, -1, 1)
 STEPS = (4, 3, 5, 2, 6, 1, 7)
+NEAR = (1, 7, 2, 6)
 MESH = pl.DeviceIdType.MESH
 F32 = jnp.float32
 BF16 = jnp.bfloat16
@@ -48,13 +50,14 @@
     parts = []
     for half in range(2):
         for group in range(GROUPS):
-            columns = pl.ds(pl.multiple_of(head * HALF, HALF) + group * HD, HD)
+            first = head * HALF if isinstance(head, int) else pl.multiple_of(head * HALF, HALF)
+            columns = pl.ds(first + group * HD, HD)
             parts.append(ref[pl.ds(half * BLOCK, BLOCK), columns])
     return jnp.concatenate(parts, axis=0)
 
 
 def columns_of(head, first):
-    return pl.ds(pl.multiple_of(head * HD, HD) + first, HD)
+    return pl.ds(head * HD + first, HD) if isinstance(head, int) else pl.ds(pl.multiple_of(head * HD, HD) + first, HD)
 
 
 def kernel(
@@ -72,8 +75,7 @@
     kv_ref,
     g_ref,
     own_ref,
-    land0,
-    land1,
+    land,
     gath,
     prob_resp,
     back_resp,
@@ -84,6 +86,7 @@
     sum_out,
     sum_land,
     in_sem,
+    near_sem,
     s1,
     r1,
     s2,
@@ -93,7 +96,6 @@
     s4,
     r4,
 ):
-    land = (land0, land1)
     row = lax.axis_index("prompt")
     column = lax.axis_index("resp")
     n_row = lax.axis_size("prompt")
@@ -105,15 +107,15 @@
     def above(step):
         return (lax.rem(row + step, n_row), column)
 
-    def heads_of(chunk):
-        return pl.ds(chunk * PER, PER)
+    def heads_of(part):
+        return pl.ds(part[0], part[1])
 
     own = pltpu.make_async_copy(pkv_hbm.at[0], own_ref, in_sem.at[0])
     own.start()
     barrier = pltpu.get_barrier_semaphore()
     for stride in STRIDES:
         pl.semaphore_signal(barrier, inc=1, device_id=beside(stride), device_id_type=MESH)
-    for step in STEPS:
+    for step in NEAR:
         pl.semaphore_signal(barrier, inc=1, device_id=above(step), device_id_type=MESH)
     loads = []
     for source, target in (
@@ -126,10 +128,11 @@
         loads[-1].start()
     own.wait()
     for head in range(KVH):
-        part = land[head // PER].at[REACH, head % PER]
+        chunk, part = next((c, p) for c, p in enumerate(PROMPT_PARTS) if p[0] <= head < p[0] + p[1])
+        part = land[chunk].at[REACH, head - part[0]]
         part[:, :HD] = own_ref[:, head * HD : (head + 1) * HD]
         part[:, HD:] = own_ref[:, KVW + head * HD : KVW + (head + 1) * HD]
-    pl.semaphore_wait(barrier, len(STRIDES) + n_row - 1)
+    pl.semaphore_wait(barrier, len(STRIDES) + len(NEAR))
 
     def to_reader(chunk, index):
         return pltpu.make_async_remote_copy(
@@ -141,9 +144,11 @@
             device_id_type=MESH,
         )
 
-    for chunk in range(CHUNKS):
+    for chunk in range(len(PROMPT_PARTS)):
         for index in range(len(STRIDES)):
             to_reader(chunk, index).start()
+    for step in NEAR:
+        pl.semaphore_signal(near_sem, inc=1, device_id=above(step), device_id_type=MESH)
     for load in loads:
         load.wait()
 
@@ -203,7 +208,7 @@
     mine = pl.ds(pl.multiple_of(row * 16, 16), 16)
 
     def along(chunk, step):
-        block = gath.at[heads_of(chunk), mine]
+        block = gath.at[heads_of(PROMPT_PARTS[chunk]), mine]
         return pltpu.make_async_remote_copy(
             src_ref=block,
             dst_ref=block,
@@ -213,18 +218,19 @@
             device_id_type=MESH,
         )
 
-    for chunk in range(CHUNKS):
+    pl.semaphore_wait(near_sem, len(NEAR))
+    for chunk in range(len(PROMPT_PARTS)):
         for index in range(len(STRIDES)):
             to_reader(chunk, index).wait_recv()
-        gath[heads_of(chunk), mine] = land[chunk][offset]
+        gath[heads_of(PROMPT_PARTS[chunk]), mine] = land[chunk][offset]
         for step in STEPS:
             along(chunk, step).start()
 
     def to_row(chunk, step):
         target = lax.rem(row + step, n_row)
         return pltpu.make_async_remote_copy(
-            src_ref=grads.at[heads_of(chunk), pl.ds(pl.multiple_of(target * 16, 16), 16)],
-            dst_ref=sums_in.at[step, heads_of(chunk)],
+            src_ref=grads.at[heads_of(GRAD_PARTS[chunk]), pl.ds(pl.multiple_of(target * 16, 16), 16)],
+            dst_ref=sums_in.at[step, heads_of(GRAD_PARTS[chunk])],
             send_sem=s3.at[chunk, step],
             recv_sem=r3.at[chunk, step],
             device_id=above(step),
@@ -254,12 +260,15 @@
         stats[head, 4:5] = delta
         return carry
 
-    for chunk in range(CHUNKS):
+    for chunk, (first, count) in enumerate(PROMPT_PARTS):
         for step in STEPS:
             along(chunk, step).wait_recv()
-        lax.fori_loop(chunk * PER, (chunk + 1) * PER, prompt, 0)
-        for step in STEPS:
-            to_row(chunk, step).start()
+        for head in range(first, first + count):
+            prompt(head, 0)
+            for part, (begin, size) in enumerate(GRAD_PARTS):
+                if begin + size == head + 1:
+                    for step in STEPS:
+                        to_row(part, step).start()
 
     def finish(head, carry):
         queries = head_rows(q_ref, head)
@@ -302,8 +311,8 @@
 
     def to_owner(chunk, index):
         return pltpu.make_async_remote_copy(
-            src_ref=sum_out.at[heads_of(chunk)],
-            dst_ref=sum_land.at[index, heads_of(chunk)],
+            src_ref=sum_out.at[heads_of(SUM_PARTS[chunk])],
+            dst_ref=sum_land.at[index, heads_of(SUM_PARTS[chunk])],
             send_sem=s4.at[chunk, index],
             recv_sem=r4.at[chunk, index],
             device_id=beside(STRIDES[index]),
@@ -311,31 +320,36 @@
         )
 
     totals = []
-    for chunk in range(CHUNKS):
-        total = grads[heads_of(chunk), mine].astype(F32)
+    for chunk, (first, count) in enumerate(SUM_PARTS):
+        heads = pl.ds(first, count)
+        for part, (begin, size) in enumerate(GRAD_PARTS):
+            if first <= begin < first + count:
+                for step in STEPS:
+                    to_row(part, step).wait_recv()
+        total = grads[heads, mine].astype(F32)
         for step in STEPS:
-            to_row(chunk, step).wait_recv()
-        for step in STEPS:
-            total = total + sums_in[step, heads_of(chunk)].astype(F32)
-        sum_out[heads_of(chunk)] = total.astype(BF16)
+            total = total + sums_in[step, heads].astype(F32)
+        sum_out[heads] = total.astype(BF16)
         for index in range(len(STRIDES)):
             to_owner(chunk, index).start()
         totals.append(jnp.where(wanted == column, total, 0.0))
-    for chunk in range(CHUNKS):
+    for chunk in range(len(PROMPT_PARTS)):
         for index in range(len(STRIDES)):
             to_reader(chunk, index).wait_send()
         for step in STEPS:
             along(chunk, step).wait_send()
-            to_row(chunk, step).wait_send()
-    for chunk in range(CHUNKS):
+    for part in range(len(GRAD_PARTS)):
+        for step in STEPS:
+            to_row(part, step).wait_send()
+    for chunk, (first, count) in enumerate(SUM_PARTS):
         total = totals[chunk]
         for index in range(len(STRIDES)):
             to_owner(chunk, index).wait()
         for index, stride in enumerate(STRIDES):
             reads = owner_ref[lax.rem(column - stride + n_col, n_col)] == column
-            total = total + jnp.where(reads, sum_land[index, heads_of(chunk)].astype(F32), 0.0)
-        for at in range(PER):
-            head = chunk * PER + at
+            total = total + jnp.where(reads, sum_land[index, pl.ds(first, count)].astype(F32), 0.0)
+        for at in range(count):
+            head = first + at
             pg_ref[:, head * HD : (head + 1) * HD] = total[at, :, :HD]
             pg_ref[:, KVW + head * HD : KVW + (head + 1) * HD] = total[at, :, HD:]
 
@@ -372,8 +386,7 @@
             pltpu.VMEM((RLEN, 2 * KVW), BF16),
             pltpu.VMEM((RLEN, QW), BF16),
             pltpu.VMEM((16, 2 * KVW), BF16),
-            pltpu.VMEM((2 * REACH + 1, PER, 16, 2 * HD), BF16),
-            pltpu.VMEM((2 * REACH + 1, PER, 16, 2 * HD), BF16),
+            [pltpu.VMEM((2 * REACH + 1, part[1], 16, 2 * HD), BF16) for part in PROMPT_PARTS],
             pltpu.VMEM((KVH, PLEN, 2 * HD), BF16),
             pltpu.VMEM((KVH, 3, BLOCK, HALF), F32),
             pltpu.VMEM((KVH, 3, BLOCK, HALF), F32),
@@ -384,14 +397,15 @@
             pltpu.VMEM((KVH, 16, 2 * HD), BF16),
             pltpu.VMEM((2 * REACH, KVH, 16, 2 * HD), BF16),
             pltpu.SemaphoreType.DMA((6,)),
-            pltpu.SemaphoreType.DMA((CHUNKS, 6)),
-            pltpu.SemaphoreType.DMA((CHUNKS, 6)),
-            pltpu.SemaphoreType.DMA((CHUNKS, 8)),
-            pltpu.SemaphoreType.DMA((CHUNKS, 8)),
-            pltpu.SemaphoreType.DMA((CHUNKS, 8)),
-            pltpu.SemaphoreType.DMA((CHUNKS, 8)),
-            pltpu.SemaphoreType.DMA((CHUNKS, 6)),
-            pltpu.SemaphoreType.DMA((CHUNKS, 6)),
+            pltpu.SemaphoreType.REGULAR,
+            pltpu.SemaphoreType.DMA((len(PROMPT_PARTS), 6)),
+            pltpu.SemaphoreType.DMA((len(PROMPT_PARTS), 6)),
+            pltpu.SemaphoreType.DMA((len(PROMPT_PARTS), 8)),
+            pltpu.SemaphoreType.DMA((len(PROMPT_PARTS), 8)),
+            pltpu.SemaphoreType.DMA((len(GRAD_PARTS), 8)),
+            pltpu.SemaphoreType.DMA((len(GRAD_PARTS), 8)),
+            pltpu.SemaphoreType.DMA((len(SUM_PARTS), 6)),
+            pltpu.SemaphoreType.DMA((len(SUM_PARTS), 6)),
         ],
         compiler_params=pltpu.CompilerParams(
             collective_id=0, has_side_effects=True, vmem_limit_bytes=40 << 20

time: 43.3 us -> 43 us (level)
  no operation moved by 1% of the time
where the time goes in v3:
time: 43 us; the launch traced here: 42.9 us
  Pallas kernels  41.6 us (97%)
  between operations  1.29 us (3%)
    pallas_call x1, Pallas kernels, shards(): pl.pallas_call(kernel, out_shape=(pltpu.VMEM((RLEN, QW), BF16), pltpu.VME...  40.4 us
    pallas_call x1, Pallas kernels, shards(): pl.pallas_call(store_kernel, out_shape=(jax.ShapeDtypeStruct(queries.shap...  1.18 us

profile of v3, /device:TPU:1, one launch (start us, length us, event | category | flops | bytes accessed | tf_op | source)
XLA Modules:
  0.0 42.9 jit_solution(9297415268913308935)
XLA Ops:
  1.3 40.4 %slot_grads.1 = (bf16[256,2048]{1,0:T(8,128)(2,1)S(1)}, bf16[256,1024]{1,0:T(8,128)(2,1)S(1)}, f32[16,1024]{1,0:T(8,128)S(1)}) custom-call(s32[1,1]{1,0:T(1,128)S(6)} %copy.9.lengths_ref, s32[64]{0:T(128)} %owner_hbm.1, bf16[1,1,256,2048]{3,2,1,0:T(8,128)(2,1)} %q_hbm.1, bf16[1,1,256,1024]{3,2,1,0:T(8,128)(2,1)} %kv_hbm.1, bf16[1,1,256,2048]{3,2,1,0:T(8,128)(2,1)} %g_hbm.1, ...), custom_call_target="tpu_custom_call" | custom-call | tf_op jit(solution)/shard_map/slot_grads/pallas_call | solution.py:374
  41.7 1.2 %store.1 = (bf16[1,1,256,2048]{3,2,1,0:T(8,128)(2,1)}, bf16[1,1,256,1024]{3,2,1,0:T(8,128)(2,1)}, f32[1,16,1024]{2,1,0:T(8,128)}) custom-call(bf16[256,2048]{1,0:T(8,128)(2,1)S(1)} %get-tuple-element.6.qg_ref, bf16[256,1024]{1,0:T(8,128)(2,1)S(1)} %get-tuple-element.7.rg_ref, f32[16,1024]{1,0:T(8,128)S(1)} %get-tuple-element.8.pg_ref), custom_call_target="tpu_custom_call" | custom-call | tf_op jit(solution)/shard_map/store/pallas_call | solution.py:416

commit v4 on v2

--- a/solution.py
+++ b/solution.py
@@ -26,6 +26,7 @@
 PER = KVH // CHUNKS
 STRIDES = (-3, 3, -2, 2, -1, 1)
 STEPS = (4, 3, 5, 2, 6, 1, 7)
+NEAR = (1, 7, 2, 6)
 MESH = pl.DeviceIdType.MESH
 F32 = jnp.float32
 BF16 = jnp.bfloat16
@@ -48,13 +49,14 @@
     parts = []
     for half in range(2):
         for group in range(GROUPS):
-            columns = pl.ds(pl.multiple_of(head * HALF, HALF) + group * HD, HD)
+            first = head * HALF if isinstance(head, int) else pl.multiple_of(head * HALF, HALF)
+            columns = pl.ds(first + group * HD, HD)
             parts.append(ref[pl.ds(half * BLOCK, BLOCK), columns])
     return jnp.concatenate(parts, axis=0)
 
 
 def columns_of(head, first):
-    return pl.ds(pl.multiple_of(head * HD, HD) + first, HD)
+    return pl.ds(head * HD + first, HD) if isinstance(head, int) else pl.ds(pl.multiple_of(head * HD, HD) + first, HD)
 
 
 def kernel(
@@ -84,6 +86,7 @@
     sum_out,
     sum_land,
     in_sem,
+    near_sem,
     s1,
     r1,
     s2,
@@ -113,7 +116,7 @@
     barrier = pltpu.get_barrier_semaphore()
     for stride in STRIDES:
         pl.semaphore_signal(barrier, inc=1, device_id=beside(stride), device_id_type=MESH)
-    for step in STEPS:
+    for step in NEAR:
         pl.semaphore_signal(barrier, inc=1, device_id=above(step), device_id_type=MESH)
     loads = []
     for source, target in (
@@ -129,7 +132,7 @@
         part = land[head // PER].at[REACH, head % PER]
         part[:, :HD] = own_ref[:, head * HD : (head + 1) * HD]
         part[:, HD:] = own_ref[:, KVW + head * HD : KVW + (head + 1) * HD]
-    pl.semaphore_wait(barrier, len(STRIDES) + n_row - 1)
+    pl.semaphore_wait(barrier, len(STRIDES) + len(NEAR))
 
     def to_reader(chunk, index):
         return pltpu.make_async_remote_copy(
@@ -144,6 +147,8 @@
     for chunk in range(CHUNKS):
         for index in range(len(STRIDES)):
             to_reader(chunk, index).start()
+    for step in NEAR:
+        pl.semaphore_signal(near_sem, inc=1, device_id=above(step), device_id_type=MESH)
     for load in loads:
         load.wait()
 
@@ -213,6 +218,7 @@
             device_id_type=MESH,
         )
 
+    pl.semaphore_wait(near_sem, len(NEAR))
     for chunk in range(CHUNKS):
         for index in range(len(STRIDES)):
             to_reader(chunk, index).wait_recv()
@@ -257,7 +263,8 @@
     for chunk in range(CHUNKS):
         for step in STEPS:
             along(chunk, step).wait_recv()
-        lax.fori_loop(chunk * PER, (chunk + 1) * PER, prompt, 0)
+        for head in range(chunk * PER, (chunk + 1) * PER):
+            prompt(head, 0)
         for step in STEPS:
             to_row(chunk, step).start()
 
@@ -384,6 +391,7 @@
             pltpu.VMEM((KVH, 16, 2 * HD), BF16),
             pltpu.VMEM((2 * REACH, KVH, 16, 2 * HD), BF16),
             pltpu.SemaphoreType.DMA((6,)),
+            pltpu.SemaphoreType.REGULAR,
             pltpu.SemaphoreType.DMA((CHUNKS, 6)),
             pltpu.SemaphoreType.DMA((CHUNKS, 6)),
             pltpu.SemaphoreType.DMA((CHUNKS, 8)),

time: 43.3 us -> 43.2 us (level)
  no operation moved by 1% of the time
where the time goes in v4:
time: 43.2 us; the launch traced here: 43.1 us
  Pallas kernels  41.8 us (97%)
  between operations  1.29 us (3%)
    pallas_call x1, Pallas kernels, shards(): pl.pallas_call(kernel, out_shape=(pltpu.VMEM((RLEN, QW), BF16), pltpu.VME...  40.6 us
    pallas_call x1, Pallas kernels, shards(): pl.pallas_call(store_kernel, out_shape=(jax.ShapeDtypeStruct(queries.shap...  1.18 us

profile of v4, /device:TPU:1, one launch (start us, length us, event | category | flops | bytes accessed | tf_op | source)
XLA Modules:
  0.0 43.1 jit_solution(13096663081076153764)
XLA Ops:
  1.3 40.6 %slot_grads.1 = (bf16[256,2048]{1,0:T(8,128)(2,1)S(1)}, bf16[256,1024]{1,0:T(8,128)(2,1)S(1)}, f32[16,1024]{1,0:T(8,128)S(1)}) custom-call(s32[1,1]{1,0:T(1,128)S(6)} %copy.9.lengths_ref, s32[64]{0:T(128)} %owner_hbm.1, bf16[1,1,256,2048]{3,2,1,0:T(8,128)(2,1)} %q_hbm.1, bf16[1,1,256,1024]{3,2,1,0:T(8,128)(2,1)} %kv_hbm.1, bf16[1,1,256,2048]{3,2,1,0:T(8,128)(2,1)} %g_hbm.1, ...), custom_call_target="tpu_custom_call" | custom-call | tf_op jit(solution)/shard_map/slot_grads/pallas_call | solution.py:367
  41.9 1.2 %store.1 = (bf16[1,1,256,2048]{3,2,1,0:T(8,128)(2,1)}, bf16[1,1,256,1024]{3,2,1,0:T(8,128)(2,1)}, f32[1,16,1024]{2,1,0:T(8,128)}) custom-call(bf16[256,2048]{1,0:T(8,128)(2,1)S(1)} %get-tuple-element.6.qg_ref, bf16[256,1024]{1,0:T(8,128)(2,1)S(1)} %get-tuple-element.7.rg_ref, f32[16,1024]{1,0:T(8,128)S(1)} %get-tuple-element.8.pg_ref), custom_call_target="tpu_custom_call" | custom-call | tf_op jit(solution)/shard_map/store/pallas_call | solution.py:410
